TPU v7x, 256 devices: a whole 4x4x8 slice. The times are simulated.
256 devices in a mesh: section: 2 (over core), rep: 8 (over y, x_lo), fsdp: 16 (over x_hi, z).
Axes of the slice: x: 4 (x_hi: 2, x_lo: 2; x = x_hi * 2 + x_lo), y: 4, z: 8, core: 2. Of those that a mesh axis runs over, the one named last changes fastest.
Arguments:
- layer_input: bfloat16 [2, 2, 8192, 8192], P('section', None, ('rep', 'fsdp')), may hold values from -600 to 600
- value_grad: bfloat16 [2, 2, 8192, 1024], P('section', None, ('rep', 'fsdp')), may hold values from -7 to 7
- value_weight: bfloat16 [2, 8192, 1024], P('section', 'fsdp'), may hold values from -2 to 2
- norm_gain: bfloat16 [2, 8192], P('section', 'fsdp'), may hold values from 0.25 to 1.75
- top_grad: bfloat16 [2, 8192, 8192], P(None, ('rep', 'fsdp')), may hold values from -6 to 6
Outputs:
- input_grad: bfloat16 [2, 2, 8192, 8192], P('section', None, ('rep', 'fsdp'))
- weight_grad: float32 [2, 8192, 1024], P('section', 'fsdp')
- gain_grad: float32 [2, 8192], P('section', 'fsdp')
All inputs are finite; a program needn't handle non-finite values.
Results may differ from a plain program's by a relative error of at most 0.0041.
Values may be sent and summed in bfloat16 or wider, within the bound.
A program may use at most 128 MiB of HBM per device.

v0:
```python
import jax
import jax.numpy as jnp
from jax import lax
from jax.sharding import PartitionSpec as P

norm_eps = 1e-05


def shifted(value, axis, steps):
    count = lax.axis_size(axis)
    initial, last = (max(0, -steps), min(count, count - steps))
    return lax.ppermute(value, axis, [(source, source + steps) for source in range(initial, last)])


def local(layer_input, value_grad, value_weight, norm_gain, top_grad):
    groups = lax.axis_size("fsdp")
    micro_count = layer_input.shape[1]
    local_rows = layer_input.shape[2]
    feature_width = layer_input.shape[3]
    total_rows = micro_count * local_rows * lax.axis_size("rep") * groups
    norm_scale = float(total_rows) ** (-0.5)
    weight_shard = value_weight[0]
    gain_shard = norm_gain[0]
    gain_column_block = gain_shard.astype(jnp.float32)
    is_upper = lax.axis_index("section") == 1
    weight_total = jnp.zeros(weight_shard.shape, jnp.float32)
    gain_total = jnp.zeros(gain_shard.shape, jnp.float32)
    results = []
    for batch_index in range(micro_count):
        layer_rows = layer_input[0, batch_index]
        grad_rows = value_grad[0, batch_index]
        columns = lax.all_to_all(layer_rows, "fsdp", split_axis=1, concat_axis=0, tiled=True)
        grads_all = lax.all_gather(grad_rows, "fsdp", axis=0, tiled=True)
        column_entries = columns.astype(jnp.float32)
        row_vals = layer_rows.astype(jnp.float32)
        scale_own = lax.rsqrt(jnp.mean(row_vals * row_vals, axis=1) + norm_eps)
        scale_every_row = lax.all_gather(scale_own, "fsdp", axis=0, tiled=True)
        centered_columns = column_entries * scale_every_row[:, None]
        normalized_input = (centered_columns * gain_column_block).astype(jnp.bfloat16)
        weight_part = lax.dot_general(
            normalized_input,
            grads_all,
            (((0,), (0,)), ((), ())),
            preferred_element_type=jnp.float32,
        )
        normalized_gradient = lax.dot_general(
            grads_all, weight_shard, (((1,), (1,)), ((), ())), preferred_element_type=jnp.float32
        )
        gain_portion = jnp.sum(normalized_gradient * centered_columns, axis=0)
        centered_gradient = normalized_gradient * gain_column_block
        row_accumulated = lax.psum(jnp.sum(centered_gradient * centered_columns, axis=1), "fsdp")
        local_cols = (
            scale_every_row[:, None]
            * (centered_gradient - centered_columns * (row_accumulated / feature_width)[:, None])
        ).astype(jnp.bfloat16)
        local_piece = lax.all_to_all(local_cols, "fsdp", split_axis=0, concat_axis=1, tiled=True)
        weight_total = weight_total + weight_part
        gain_total = gain_total + gain_portion
        local_f = local_piece.astype(jnp.float32)
        upper = (top_grad[batch_index].astype(jnp.float32) + local_f).astype(jnp.bfloat16)
        passed = shifted(upper, "section", -1)
        lower = (passed.astype(jnp.float32) + local_f).astype(jnp.bfloat16)
        results.append(jnp.where(is_upper, upper, lower))
    weight_total, gain_total = lax.psum((weight_total, gain_total), "rep")
    input_grad = jnp.stack(results)[None]
    return (input_grad, (weight_total * norm_scale)[None], (gain_total * norm_scale)[None])


def solution(mesh):
    return jax.shard_map(
        local,
        mesh=mesh,
        in_specs=(
            P("section", None, ("rep", "fsdp"), None),
            P("section", None, ("rep", "fsdp"), None),
            P("section", "fsdp", None),
            P("section", "fsdp"),
            P(None, ("rep", "fsdp"), None),
        ),
        out_specs=(
            P("section", None, ("rep", "fsdp"), None),
            P("section", "fsdp", None),
            P("section", "fsdp"),
        ),
        check_vma=False,
    )
```

profile of v0, /device:TPU:4, one launch (start us, length us, event | category | flops | bytes accessed | tf_op | source)
XLA Modules:
  0.0 406.1 jit_solution(1689640947787552370)
XLA Ops:
  7.2 0.0 copy-start
  7.2 0.0 all-gather.7.cloned.1.call-start
  7.2 1.8 fusion.20
  9.0 0.0 all-gather.7.cloned.1.call-update
  9.0 1.7 fusion.19
  10.7 0.4 copy.15
  11.1 1.5 copy.10
  12.6 11.4 %all-to-all-start.2 = ((bf16[64,16,512]{2,0,1:T(8,128)(2,1)}), bf16[64,16,512]{2,0,1:T(8,128)(2,1)}, u32[]{:S(2)}, u32[]{:S(2)}) async-start(bf16[64,16,512]{2,0,1:T(8,128)(2,1)} %copy.10), calls=%async_computation.2 | async-start | bytes 2097152 | tf_op jit(solution)/shard_map/all_to_all | solution.py:32
  24.1 0.0 all-gather.5.cloned.1.call-start
  24.1 0.7 all-gather.5.cloned.1.call-update
  24.8 0.4 copy.14
  25.2 0.0 copy-start.8
  25.2 0.0 copy-start.10
  25.2 0.0 copy-start.3
  25.2 1.5 copy.8
  26.7 27.3 %all-to-all-done.2 = bf16[64,16,512]{2,0,1:T(8,128)(2,1)} async-done(((bf16[64,16,512]{2,0,1:T(8,128)(2,1)}), bf16[64,16,512]{2,0,1:T(8,128)(2,1)}, u32[]{:S(2)}, u32[]{:S(2)}) %all-to-all-start.2) | async-done | bytes 1048608 | tf_op jit(solution)/shard_map/all_to_all | solution.py:32
  54.1 6.9 %all-to-all-start = ((bf16[64,16,512]{2,0,1:T(8,128)(2,1)}), bf16[64,16,512]{2,0,1:T(8,128)(2,1)}, u32[]{:S(2)}, u32[]{:S(2)}) async-start(bf16[64,16,512]{2,0,1:T(8,128)(2,1)} %copy.8), calls=%async_computation | async-start | bytes 2097152 | tf_op jit(solution)/shard_map/all_to_all | solution.py:32
  60.9 0.0 copy-done.8
  60.9 0.0 copy-done.10
  61.0 0.6 dynamic-slice
  62.2 0.0 copy-done.3
  62.2 0.5 multiply_reduce_fusion.5
  62.7 0.1 rsqrt_dynamic-update-slice_fusion
  62.9 0.1 rsqrt_dynamic-update-slice_fusion.1
  63.0 57.7 %all-reduce.3 = (f32[1024]{0:T(1024)S(1)}, f32[1024]{0:T(1024)S(1)}) all-reduce(f32[1024]{0:T(1024)S(1)} %rsqrt_dynamic-update-slice_fusion, f32[1024]{0:T(1024)S(1)} %rsqrt_dynamic-update-slice_fusion.1), channel_id=1, replica_groups=mesh['section'=2,'rep'=8,'fsdp'=16] {'fsdp'}, use_global_device_ids=true, to_apply=%add.1 | all-reduce | flops 2048 | bytes 16384
  120.7 0.0 all-gather.7.cloned.1.call-done
  120.7 0.0 copy-done
  120.7 2.9 fusion.4
  123.6 0.0 copy-start.6
  123.6 0.0 all-to-all-done
  123.6 71.3 %all-gather.5.cloned.1.call-done = bf16[1,1,1024,1024]{3,2,1,0:T(8,128)(2,1)} async-done(((bf16[1,1,64,1024]{3,2,1,0:T(8,128)(2,1)}), bf16[1,1,1024,1024]{3,2,1,0:T(8,128)(2,1)}) %all-gather.5.cloned.1.call-update) | async-done | bytes 2097168 | tf_op jit(solution)/shard_map/all_gather | solution.py:33
  195.0 5.0 %multiply_reduce_fusion.1 = (f32[512]{0:T(512)S(1)}, f32[1024]{0:T(1024)S(1)}, f32[1024]{0:T(1024)S(1)}, f32[512]{0:T(512)S(1)}, f32[1024,512]{1,0:T(8,128)}) fusion(bf16[64,16,512]{2,0,1:T(8,128)(2,1)} %all-to-all-done, f32[1024]{0:T(1024)S(1)} %get-tuple-element.12, f32[512]{0:T(512)S(1)} %bitcast.95, f32[1024,512]{1,0:T(8,128)S(1)} %fusion.4, ...), kind=kOutput, calls=%fused_computation.18 | convolution fusion | flops 1081078784 | bytes 9459712 | tf_op jit(solution)/shard_map/dot_general | solution.py:46
  200.0 0.0 copy-done.6
  200.0 41.2 %all-reduce.2 = (f32[1024]{0:T(1024)S(1)}, f32[1024]{0:T(1024)S(1)}) all-reduce(f32[1024]{0:T(1024)S(1)} %get-tuple-element.27, f32[1024]{0:T(1024)S(1)} %get-tuple-element.6), channel_id=1, replica_groups=mesh['section'=2,'rep'=8,'fsdp'=16] {'fsdp'}, use_global_device_ids=true, to_apply=%region_5.6 | all-reduce | flops 2048 | bytes 16384 | tf_op jit(solution)/shard_map/psum | solution.py:51
  241.2 4.5 %multiply_convert_fusion.1 = (bf16[1024,512]{1,0:T(8,128)(2,1)}, bf16[1024,512]{1,0:T(8,128)(2,1)}, bf16[1024,512]{1,0:T(8,128)(2,1)S(1)}, bf16[1024,512]{1,0:T(8,128)(2,1)S(1)}) fusion(bf16[64,16,512]{2,0,1:T(8,128)(2,1)} %all-to-all-done, f32[512]{0:T(512)S(1)} %bitcast.96, f32[1024]{0:T(1024)S(1)} %get-tuple-element.12, f32[1024]{0:T(1024)S(1)} %get-tuple-element.31, ...), kind=kLoop, calls=%fused_computation.21 | loop fusion | flops 9437184 | bytes 10504192 | tf_op jit(solution)/shard_map/convert_element_type | solution.py:39
  245.7 21.5 %all_to_all.52 = bf16[16,64,512]{2,1,0:T(8,128)(2,1)S(1)} all-to-all(bf16[16,64,512]{2,1,0:T(8,128)(2,1)S(1)} %bitcast.90), channel_id=1, replica_groups=mesh['section'=2,'rep'=8,'fsdp'=16] {'fsdp'}, dimensions={0} | all-to-all | bytes 2097152 | tf_op jit(solution)/shard_map/all_to_all | solution.py:56
  267.1 8.3 %all-to-all-start.1 = ((bf16[16,64,512]{2,1,0:T(8,128)(2,1)}), bf16[16,64,512]{2,1,0:T(8,128)(2,1)}, u32[]{:S(2)}, u32[]{:S(2)}) async-start(bf16[16,64,512]{2,1,0:T(8,128)(2,1)} %bitcast.7), calls=%async_computation.1 | async-start | bytes 2097152 | tf_op jit(solution)/shard_map/all_to_all | solution.py:56
  275.5 0.0 all-reduce.6.cloned.1.call-start
  275.5 0.0 copy-start.7
  275.5 0.0 copy-start.9
  275.5 3.0 fusion.2
  278.5 0.0 copy-done.7
  278.5 2.6 fusion.10
  281.1 0.0 all-reduce.6.cloned.1.call-update
  281.2 0.3 convert_bitcast_fusion
  281.4 0.2 copy.13
  281.7 8.7 %all-to-all-done.1 = bf16[16,64,512]{2,1,0:T(8,128)(2,1)} async-done(((bf16[16,64,512]{2,1,0:T(8,128)(2,1)}), bf16[16,64,512]{2,1,0:T(8,128)(2,1)}, u32[]{:S(2)}, u32[]{:S(2)}) %all-to-all-start.1) | async-done | bytes 1048608 | tf_op jit(solution)/shard_map/all_to_all | solution.py:56
  290.4 1.5 convert_bitcast_fusion.1
  291.9 0.0 copy-start.4
  291.9 0.2 copy.12
  292.1 0.0 copy-start.1
  292.2 2.1 copy-done.4
  294.3 1.7 fusion.1
  296.0 0.0 copy-done.1
  296.0 1.3 collective-permute-start
  297.3 1.3 collective-permute-start.1
  298.6 20.8 %psum.31 = f32[512]{0:T(512)S(1)} all-reduce(f32[512]{0:T(512)S(1)} %add.39), channel_id=1, replica_groups=mesh['section'=2,'rep'=8,'fsdp'=16] {'rep'}, use_global_device_ids=true, to_apply=%region_9.10 | all-reduce | flops 512 | bytes 4096 | tf_op jit(solution)/shard_map/psum | solution.py:64
  319.4 0.6 broadcast_multiply_fusion.2
  320.0 72.4 %all-reduce.6.cloned.1.call-done = f32[512,1024]{1,0:T(8,128)} async-done(((f32[512,1024]{1,0:T(8,128)}), f32[512,1024]{1,0:T(8,128)}) %all-reduce.6.cloned.1.call-update) | async-done | bytes 2097168 | tf_op jit(solution)/shard_map/psum | solution.py:64
  392.4 3.4 multiply_bitcast_fusion
  395.7 0.0 collective-permute-done
  395.7 0.0 collective-permute-done.1
  395.7 2.4 fusion.14
  398.1 1.5 maximum_bitcast_fusion
  (10 shorter events, 0.0 us)
Async XLA Ops:
  7.2 113.6 %copy-start = (bf16[1,512,1024]{2,1,0:T(8,128)(2,1)S(1)}, bf16[1,512,1024]{2,1,0:T(8,128)(2,1)}, u32[]{:S(2)}) copy-start(bf16[1,512,1024]{2,1,0:T(8,128)(2,1)} %param.7) | copy-start | bytes 3145732
  7.2 113.5 %all-gather.7.cloned.1.call-start = ((), (), s32[]{:S(2)}) async-start(), calls=%async_computation.6 | async-start | bytes 2228224 | tf_op jit(solution)/shard_map/all_gather | solution.py:33
  12.6 41.5 %all-to-all-start.2 = ((bf16[64,16,512]{2,0,1:T(8,128)(2,1)}), bf16[64,16,512]{2,0,1:T(8,128)(2,1)}, u32[]{:S(2)}, u32[]{:S(2)}) async-start(bf16[64,16,512]{2,0,1:T(8,128)(2,1)} %copy.10), calls=%async_computation.2 | async-start | bytes 2097152 | tf_op jit(solution)/shard_map/all_to_all | solution.py:32
  24.1 170.9 %all-gather.5.cloned.1.call-start = ((), (), s32[]{:S(2)}) async-start(), calls=%async_computation.5 | async-start | bytes 2228224 | tf_op jit(solution)/shard_map/all_gather | solution.py:33
  25.2 35.8 %copy-start.8 = (bf16[1,512]{1,0:T(2,128)(2,1)S(1)}, bf16[1,512]{1,0:T(2,128)(2,1)}, u32[]{:S(2)}) copy-start(bf16[1,512]{1,0:T(2,128)(2,1)} %param.8) | copy-start | bytes 3076
  25.2 35.8 %copy-start.10 = (u32[256]{0:T(256)S(1)}, u32[256]{0:T(256)}, u32[]{:S(2)}) copy-start(u32[256]{0:T(256)} %constant.29) | copy-start | bytes 3076
  25.2 37.0 %copy-start.3 = (bf16[1,2,64,8192]{3,2,1,0:T(8,128)(2,1)S(1)}, bf16[1,2,64,8192]{3,2,1,0:T(8,128)(2,1)}, u32[]{:S(2)}) copy-start(bf16[1,2,64,8192]{3,2,1,0:T(8,128)(2,1)} %param.5) | copy-start | bytes 6291460
  54.1 69.6 %all-to-all-start = ((bf16[64,16,512]{2,0,1:T(8,128)(2,1)}), bf16[64,16,512]{2,0,1:T(8,128)(2,1)}, u32[]{:S(2)}, u32[]{:S(2)}) async-start(bf16[64,16,512]{2,0,1:T(8,128)(2,1)} %copy.8), calls=%async_computation | async-start | bytes 2097152 | tf_op jit(solution)/shard_map/all_to_all | solution.py:32
  123.6 76.4 %copy-start.6 = (f32[1024,512]{1,0:T(8,128)}, f32[1024,512]{1,0:T(8,128)S(1)}, u32[]{:S(2)}) copy-start(f32[1024,512]{1,0:T(8,128)S(1)} %fusion.4) | copy-start | bytes 6291460
  267.1 23.3 %all-to-all-start.1 = ((bf16[16,64,512]{2,1,0:T(8,128)(2,1)}), bf16[16,64,512]{2,1,0:T(8,128)(2,1)}, u32[]{:S(2)}, u32[]{:S(2)}) async-start(bf16[16,64,512]{2,1,0:T(8,128)(2,1)} %bitcast.7), calls=%async_computation.1 | async-start | bytes 2097152 | tf_op jit(solution)/shard_map/all_to_all | solution.py:56
  275.5 116.9 %all-reduce.6.cloned.1.call-start = ((), (), s32[]{:S(2)}) async-start(), calls=%async_computation.4 | async-start | bytes 4194304 | tf_op jit(solution)/shard_map/psum | solution.py:64
  275.5 3.0 copy-start.7
  275.5 3.0 copy-start.9
  291.9 2.4 copy-start.4
  292.1 3.9 copy-start.1
  296.0 99.7 %collective-permute-start = (bf16[64,8192]{1,0:T(8,128)(2,1)}, bf16[64,8192]{1,0:T(8,128)(2,1)}, u32[]{:S(2)}, u32[]{:S(2)}) collective-permute-start(bf16[64,8192]{1,0:T(8,128)(2,1)} %get-tuple-element.15), channel_id=1, source_target_pairs={{128,0},{129,1},{130,2},{131,3},{132,4},{133,5},{134,6},{135,7},{1... | collective-permute-start | bytes 3145736 | tf_op jit(solution)/shard_map/ppermute | solution.py:12
  297.3 98.4 %collective-permute-start.1 = (bf16[64,8192]{1,0:T(8,128)(2,1)}, bf16[64,8192]{1,0:T(8,128)(2,1)}, u32[]{:S(2)}, u32[]{:S(2)}) collective-permute-start(bf16[64,8192]{1,0:T(8,128)(2,1)} %get-tuple-element.16), channel_id=1, source_target_pairs={{128,0},{129,1},{130,2},{131,3},{132,4},{133,5},{134,6},{135,7},{1... | collective-permute-start | bytes 3145736 | tf_op jit(solution)/shard_map/ppermute | solution.py:12
  392.4 3.4 copy-start.2
  392.4 3.4 copy-start.5
Sparse Core Ops, SparseCore 0:
  10.6 100.5 all-gather.6
  113.8 81.1 all-gather.4
  281.3 111.0 all-reduce.5
where the time goes:
time: 408 us; the launch traced here: 406 us
  waiting for transfers between devices  181 us (44%)
  blocking collectives  141 us (35%)
  starting transfers between devices  29.3 us (7%)
  other arithmetic  16.5 us (4%)
  between operations  14.7 us (4%)
  matrix products  13.5 us (3%)
  local copies, waits for them, and re-layouts  10.5 us (3%)
    psum x1, waiting for transfers between devices, local(): weight_total, gain_total = lax.psum((weight_total, gain_total), 'rep')  72.4 us
    all_gather x2, waiting for transfers between devices, local(): grads_all = lax.all_gather(grad_rows, 'fsdp', axis=0, tiled=True)  71.4 us
    unnamed x1, blocking collectives  57.7 us
    psum x1, blocking collectives, local(): lax.psum(jnp.sum(centered_gradient * centered_columns, axis=1), 'fsdp')  41.2 us
    all_to_all x2, waiting for transfers between devices, local(): lax.all_to_all(layer_rows, 'fsdp', split_axis=1, concat_axis=0, tiled=True)  27.3 us
    all_to_all x1, blocking collectives, local(): lax.all_to_all(local_cols, 'fsdp', split_axis=0, concat_axis=1, tiled=True)  21.5 us
    psum x1, blocking collectives, local(): weight_total, gain_total = lax.psum((weight_total, gain_total), 'rep')  20.8 us
    all_to_all x2, starting transfers between devices, local(): lax.all_to_all(layer_rows, 'fsdp', split_axis=1, concat_axis=0, tiled=True)  18.3 us
  transfers between devices with their start and end apart: 8, of which 4 were waited for; matrix products, arithmetic and copies ran while one was open for 6% of the time, Pallas kernels for 0%

commit v1 on v0

v1 whole, which is shorter than its diff:
```python
import functools

import jax
import jax.numpy as jnp
from jax import lax
from jax.experimental import pallas as pl
from jax.experimental.pallas import tpu as pltpu
from jax.sharding import PartitionSpec as P

NORM_EPS = 1e-05
MESH = pl.DeviceIdType.MESH
NZ = 8
NY = 4
F32 = jnp.float32
BF16 = jnp.bfloat16


def remote(src, dst, send_sem, recv_sem, device):
    return pltpu.make_async_remote_copy(
        src_ref=src, dst_ref=dst, send_sem=send_sem, recv_sem=recv_sem, device_id=device, device_id_type=MESH
    )


def kernel(
    norm_scale,
    x_hbm, g_hbm, w_hbm, gain_ref, top_hbm,
    ig_ref, wg_ref, gg_ref,
    xbuf, topbuf, wown, gain_src, gain_all, scale_buf, nb, xr, gr, wr, pb, ra, sb, rb, ag, db, dr, upper, ggbuf,
    local_sem, gain_ss, gain_rs, g_ss, g_rs, x_ss, x_rs, w_ss, w_rs, w2_ss, w2_rs,
    a_ss, a_rs, b_ss, b_rs, c_ss, c_rs, q_ss, q_rs, d_ss, d_rs, u_ss, u_rs,
):
    tokens, width = xbuf.shape
    half = tokens // 2
    blocks, _, bw = nb.shape
    vw = gr.shape[1]
    rows = sb.shape[1]
    rep = lax.axis_index("rep")
    fs = lax.axis_index("fsdp")
    sec = lax.axis_index("section")
    xl, y, xh, z = rep % 2, rep // 2, fs // NZ, fs % NZ
    yp = (y + 1 + 2 * ((y + sec) % 2)) % NY
    zp = (z + 1 + (NZ - 2) * ((z + sec) % 2)) % NZ
    jy, jz = y % 2, z % 2
    me = xh * 4 + jy * 2 + jz

    def zprime(ky, kz, i):
        return kz + 2 * ((2 * ky + i + 2 * sec) % 4)

    def member(flip):
        fh, fy, fz = flip // 4, (flip // 2) % 2, flip % 2
        mxl = xl + fh * (1 - 2 * xl)
        mxh = xh + fh * (1 - 2 * xh)
        my = y + fy * (yp - y)
        mz = z + fz * (zp - z)
        label = (mxh, my % 2, mz % 2)
        device = {"rep": my * 2 + mxl, "fsdp": mxh * NZ + mz}
        return device, label, label[0] * 4 + label[1] * 2 + label[2]

    def block(label, i):
        return label[0] * NZ + zprime(label[1], label[2], i)

    xcopy = pltpu.make_async_copy(x_hbm, xbuf, local_sem.at[0])
    xcopy.start()
    tcopy = pltpu.make_async_copy(top_hbm, topbuf, local_sem.at[1])
    tcopy.start()
    wcopy = pltpu.make_async_copy(w_hbm, wown, local_sem.at[2])
    wcopy.start()
    my_rows = pl.ds(pl.multiple_of(me * tokens, tokens), tokens)
    gcopy = pltpu.make_async_copy(g_hbm, gr.at[my_rows], local_sem.at[3])
    gcopy.start()
    gain_f = jnp.broadcast_to(gain_ref[...].astype(F32), gain_src.shape)
    gain_src[...] = gain_f
    gain_all[fs] = gain_f

    barrier = pltpu.get_barrier_semaphore()

    def hello(device):
        pl.semaphore_signal(barrier, inc=1, device_id=device, device_id_type=MESH)

    @pl.loop(1, 8)
    def _(f):
        hello(member(f)[0])
        hello({"rep": (rep + f) % 8})

    @pl.loop(1, 16)
    def _(k):
        hello({"fsdp": (fs + k) % 16})

    hello({"section": 1 - sec})
    pl.semaphore_wait(barrier, 7 + 7 + 15 + 1)

    @pl.loop(1, 16)
    def _(k):
        remote(gain_src, gain_all.at[fs], gain_ss.at[k], gain_rs.at[fs], {"fsdp": (fs + k) % 16}).start()

    def g_copy(n, f, owner, src):
        dst = gr.at[pl.ds(pl.multiple_of(owner * tokens, tokens), tokens)]
        return remote(src, dst, g_ss.at[n], g_rs.at[owner], member(f)[0])

    for n, f in enumerate((4, 1, 2, 3)):
        g_copy(n, f, me, g_hbm).start()

    root = z == zprime(jy, jz, xl)
    wh = w_hbm.shape[0] // 2
    w_parts = [pl.ds(0, wh), pl.ds(wh, wh)]

    def w_copy(n, p):
        return remote(
            w_hbm.at[w_parts[p]], wr.at[xl, w_parts[p]], w_ss.at[n, p], w_rs.at[p],
            {"fsdp": xh * NZ + (z + (2, 6, 4)[n]) % NZ},
        )

    def w_local(p):
        return pltpu.make_async_copy(w_hbm.at[w_parts[p]], wr.at[xl, w_parts[p]], local_sem.at[4 + p])

    @pl.when(root)
    def _():
        for p in range(2):
            w_local(p).start()
            for n in range(3):
                w_copy(n, p).start()

    xcopy.wait()

    def columns(b):
        return pl.ds(pl.multiple_of(b * bw, bw), bw)

    def squares(b, acc):
        v = xbuf[:, columns(b)].astype(F32)
        v = v * v
        for k in range(bw // 128):
            acc = acc + v[:, k * 128 : (k + 1) * 128]
        return acc

    acc = lax.fori_loop(0, blocks, squares, jnp.zeros((tokens, 128), F32))
    scale = lax.rsqrt(jnp.sum(acc, axis=1, keepdims=True) / width + NORM_EPS)
    scale_buf[...] = jnp.broadcast_to(scale, scale_buf.shape)

    @pl.loop(1, 16)
    def _(k):
        src = (fs + k) % 16
        remote(gain_src, gain_all.at[src], gain_ss.at[k], gain_rs.at[src], {"fsdp": src}).wait_recv()

    @pl.loop(0, blocks)
    def _(b):
        v = xbuf[:, columns(b)].astype(F32) * scale_buf[:, 0:1]
        nb[b] = (v * gain_all[b, 0:1, :]).astype(BF16)

    def x_copy(f, i):
        device, label, _ = member(f)
        return remote(nb.at[block(label, i)], xr.at[i, my_rows], x_ss.at[f, i], x_rs.at[me, i], device)

    for i in range(2):
        @pl.loop(1, 8)
        def _(f):
            x_copy(f, i).start()

    for i in range(2):
        xr[i, my_rows] = nb[block((xh, jy, jz), i)]

    other = (me + 4) % 8
    other_rows = pl.ds(pl.multiple_of(other * tokens, tokens), tokens)
    g_copy(0, 4, other, g_hbm).wait_recv()
    for n, f in enumerate((1, 2, 3)):
        g_copy(4 + n, f, other, gr.at[other_rows]).start()

    gcopy.wait()

    @pl.loop(1, 8)
    def _(f):
        m = member(f)[2]

        @pl.when(f != 4)
        def _():
            g_copy(0, 4, m, g_hbm).wait_recv()

    def wgrad(i):
        @pl.loop(1, 8)
        def _(f):
            m = member(f)[2]
            dst = xr.at[i, pl.ds(pl.multiple_of(m * tokens, tokens), tokens)]
            remote(nb.at[0], dst, x_ss.at[f, i], x_rs.at[m, i], {"section": sec}).wait_recv()

        part = lax.dot_general(xr[i], gr[...], (((0,), (0,)), ((), ())), preferred_element_type=F32)
        pb[i] = part.astype(BF16)

        @pl.loop(1, 8)
        def _(k):
            c = (rep + k) % 8
            a_copy(k, i, c).start()

        ra[rep, i] = pb[i, pl.ds(pl.multiple_of(rep * rows, rows), rows)]

    def a_copy(k, i, c):
        return remote(
            pb.at[i, pl.ds(pl.multiple_of(c * rows, rows), rows)], ra.at[rep, i],
            a_ss.at[k, i], a_rs.at[rep, i], {"rep": c},
        )

    for i in range(2):
        wgrad(i)

    def w_swap(p):
        return remote(
            wr.at[xl, w_parts[p]], wr.at[xl, w_parts[p]], w2_ss.at[p], w2_rs.at[p], {"rep": y * 2 + 1 - xl}
        )

    for p in range(2):
        @pl.when(root)
        def _():
            w_local(p).wait()

        @pl.when(jnp.logical_not(root))
        def _():
            w_copy(0, p).wait_recv()

        w_swap(p).start()

    @pl.loop(1, 8)
    def _(k):
        c = (rep + k) % 8
        for i in range(2):
            remote(pb.at[i, pl.ds(0, rows)], ra.at[c, i], a_ss.at[k, i], a_rs.at[c, i], {"rep": c}).wait_recv()

    for ky in range(2):
        for i in range(2):
            total = ra[2 * ky, i].astype(F32) + ra[2 * ky + 1, i].astype(F32)
            total = total + (ra[2 * ky + 4, i].astype(F32) + ra[2 * ky + 5, i].astype(F32))
            sb[2 * ky + i] = total.astype(BF16)

    zk = z // 2

    def b_copy(k):
        slot = (zk + k) % 4
        return remote(
            sb.at[(slot + 2 * sec) % 4], rb.at[zk], b_ss.at[k], b_rs.at[zk], {"fsdp": xh * NZ + jz + 2 * slot}
        )

    for k in range(1, 4):
        b_copy(k).start()
    rb[zk] = sb[(zk + 2 * sec) % 4]

    for p in range(2):
        remote(
            wr.at[1 - xl, w_parts[p]], wr.at[1 - xl, w_parts[p]], w2_ss.at[p], w2_rs.at[p], {"section": sec}
        ).wait_recv()

    def d_copy(f, i):
        device, _, m = member(f)
        return remote(
            db.at[i, pl.ds(pl.multiple_of(m * tokens, tokens), tokens)], dr.at[block((xh, jy, jz), i)],
            d_ss.at[f, i], d_rs.at[block((xh, jy, jz), i)], device,
        )

    for i in range(2):
        back = lax.dot_general(gr[...], wr[i], (((1,), (1,)), ((), ())), preferred_element_type=F32)
        db[i] = back.astype(BF16)

        @pl.loop(1, 8)
        def _(f):
            d_copy(f, i).start()

        dr[block((xh, jy, jz), i)] = db[i, my_rows]

    for k in range(1, 4):
        slot = (zk + k) % 4
        remote(sb.at[0], rb.at[slot], b_ss.at[k], b_rs.at[slot], {"section": sec}).wait_recv()
    total = (rb[0].astype(F32) + rb[1].astype(F32)) + (rb[2].astype(F32) + rb[3].astype(F32))
    total = total * norm_scale
    ag[rep] = total.astype(BF16)
    wcopy.wait()
    gg = jnp.sum(total * wown[pl.ds(pl.multiple_of(rep * rows, rows), rows)].astype(F32), axis=1, keepdims=True)
    gg = jnp.broadcast_to(jnp.concatenate([gg, gg], axis=0), (2 * rows, 128))
    ggbuf[rep] = gg.T[0:8]

    def c_copy(k, c):
        return remote(ag.at[rep], ag.at[rep], c_ss.at[k], c_rs.at[rep], {"rep": c})

    def q_copy(k, c):
        return remote(ggbuf.at[rep], ggbuf.at[rep], q_ss.at[k], q_rs.at[rep], {"rep": c})

    @pl.loop(1, 8)
    def _(k):
        c_copy(k, (rep + k) % 8).start()
        q_copy(k, (rep + k) % 8).start()

    tcopy.wait()

    @pl.loop(1, 8)
    def _(f):
        label = member(f)[1]
        for i in range(2):
            b = block(label, i)
            remote(db.at[0, pl.ds(0, tokens)], dr.at[b], d_ss.at[f, i], d_rs.at[b], {"section": sec}).wait_recv()

    def u_copy(mi):
        part = pl.ds(mi * half, half)
        return remote(ig_ref.at[part], upper.at[part], u_ss.at[mi], u_rs.at[mi], {"section": 0})

    for mi in range(2):
        part = pl.ds(mi * half, half)

        def dots(b, acc):
            v = dr[b, part].astype(F32) * gain_all[b, 0:1, :]
            v = v * (xbuf[part, columns(b)].astype(F32) * scale_buf[part, 0:1])
            for k in range(bw // 128):
                acc = acc + v[:, k * 128 : (k + 1) * 128]
            return acc

        acc = lax.fori_loop(0, blocks, dots, jnp.zeros((half, 128), F32))
        avg = jnp.sum(acc, axis=1, keepdims=True) / width

        def finish(addend):
            @pl.loop(0, blocks)
            def _(b):
                sc = scale_buf[part, 0:1]
                v = dr[b, part].astype(F32) * gain_all[b, 0:1, :]
                v = sc * (v - xbuf[part, columns(b)].astype(F32) * sc * avg)
                v = v.astype(BF16).astype(F32)
                ig_ref[part, columns(b)] = (addend[part, columns(b)].astype(F32) + v).astype(BF16)

        @pl.when(sec == 1)
        def _():
            finish(topbuf)
            u_copy(mi).start()

        @pl.when(sec == 0)
        def _():
            u_copy(mi).wait_recv()
            finish(upper)

    @pl.loop(1, 8)
    def _(k):
        c = (rep + k) % 8
        remote(ag.at[c], ag.at[c], c_ss.at[k], c_rs.at[c], {"rep": c}).wait_recv()
        remote(ggbuf.at[c], ggbuf.at[c], q_ss.at[k], q_rs.at[c], {"rep": c}).wait_recv()

    for c in range(8):
        wg_ref[c * rows : (c + 1) * rows] = ag[c].astype(F32)
        gg_ref[c : c + 1] = ggbuf[c, 0:1]

    @pl.loop(1, 16)
    def _(k):
        remote(gain_src, gain_all.at[fs], gain_ss.at[k], gain_rs.at[fs], {"fsdp": (fs + k) % 16}).wait_send()

    for n, f in enumerate((4, 1, 2, 3)):
        g_copy(n, f, me, g_hbm).wait_send()
    for n, f in enumerate((1, 2, 3)):
        g_copy(4 + n, f, other, gr.at[other_rows]).wait_send()

    @pl.when(root)
    def _():
        for p in range(2):
            for n in range(3):
                w_copy(n, p).wait_send()

    for p in range(2):
        w_swap(p).wait_send()

    @pl.loop(1, 8)
    def _(k):
        c = (rep + k) % 8
        for i in range(2):
            x_copy(k, i).wait_send()
            a_copy(k, i, c).wait_send()
            d_copy(k, i).wait_send()
        c_copy(k, c).wait_send()
        q_copy(k, c).wait_send()

    for k in range(1, 4):
        b_copy(k).wait_send()

    @pl.when(sec == 1)
    def _():
        for mi in range(2):
            u_copy(mi).wait_send()


def local(layer_input, value_grad, value_weight, norm_gain, top_grad):
    reps, groups = lax.axis_size("rep"), lax.axis_size("fsdp")
    _, micro, rows, width = layer_input.shape
    vw = value_grad.shape[3]
    tokens = micro * rows
    bw = value_weight.shape[1]
    blocks = width // bw
    slice_rows = bw // reps
    norm_scale = float(tokens * reps * groups) ** (-0.5)
    any_spec = pl.BlockSpec(memory_space=pl.ANY)
    vmem = pl.BlockSpec(memory_space=pltpu.VMEM)
    dma = pltpu.SemaphoreType.DMA
    grad, wgrad, ggrad = pl.pallas_call(
        functools.partial(kernel, norm_scale),
        out_shape=(
            jax.ShapeDtypeStruct((tokens, width), BF16),
            jax.ShapeDtypeStruct((bw, vw), F32),
            jax.ShapeDtypeStruct((8, 128), F32),
        ),
        in_specs=[any_spec, any_spec, any_spec, vmem, any_spec],
        out_specs=(vmem, vmem, vmem),
        scratch_shapes=[
            pltpu.VMEM((tokens, width), BF16),
            pltpu.VMEM((tokens, width), BF16),
            pltpu.VMEM((bw, vw), BF16),
            pltpu.VMEM((8, bw), F32),
            pltpu.VMEM((blocks, 8, bw), F32),
            pltpu.VMEM((tokens, 128), F32),
            pltpu.VMEM((blocks, tokens, bw), BF16),
            pltpu.VMEM((2, 8 * tokens, bw), BF16),
            pltpu.VMEM((8 * tokens, vw), BF16),
            pltpu.VMEM((2, bw, vw), BF16),
            pltpu.VMEM((2, bw, vw), BF16),
            pltpu.VMEM((8, 2, slice_rows, vw), BF16),
            pltpu.VMEM((4, slice_rows, vw), BF16),
            pltpu.VMEM((4, slice_rows, vw), BF16),
            pltpu.VMEM((8, slice_rows, vw), BF16),
            pltpu.VMEM((2, 8 * tokens, bw), BF16),
            pltpu.VMEM((blocks, tokens, bw), BF16),
            pltpu.VMEM((tokens, width), BF16),
            pltpu.VMEM((8, 8, 128), F32),
            dma((6,)),
            dma((16,)), dma((16,)),
            dma((7,)), dma((8,)),
            dma((8, 2)), dma((8, 2)),
            dma((3, 2)), dma((2,)), dma((2,)), dma((2,)),
            dma((8, 2)), dma((8, 2)),
            dma((4,)), dma((4,)),
            dma((8,)), dma((8,)), dma((8,)), dma((8,)),
            dma((8, 2)), dma((16,)),
            dma((2,)), dma((2,)),
        ],
        compiler_params=pltpu.CompilerParams(
            collective_id=0, has_side_effects=True, vmem_limit_bytes=60 * 1024 * 1024
        ),
        name="relay",
    )(
        layer_input.reshape(tokens, width),
        value_grad.reshape(tokens, vw),
        value_weight[0],
        norm_gain,
        top_grad.reshape(tokens, width),
    )
    gain_grad = ggrad[:, :slice_rows].reshape(1, bw) / norm_gain.astype(F32)
    return grad.reshape(layer_input.shape), wgrad[None], gain_grad


def solution(mesh):
    return jax.shard_map(
        local,
        mesh=mesh,
        in_specs=(
            P("section", None, ("rep", "fsdp"), None),
            P("section", None, ("rep", "fsdp"), None),
            P("section", "fsdp", None),
            P("section", "fsdp"),
            P(None, ("rep", "fsdp"), None),
        ),
        out_specs=(
            P("section", None, ("rep", "fsdp"), None),
            P("section", "fsdp", None),
            P("section", "fsdp"),
        ),
        check_vma=False,
    )
```

time: 408 us -> 160 us (0.39)
  waiting for transfers between devices: 181 us -> 0 us
  Pallas kernels: 0 us -> 153 us
  blocking collectives: 141 us -> 0 us
  starting transfers between devices: 29.3 us -> 0 us
  other arithmetic: 16.5 us -> 0.59 us
  between operations: 14.7 us -> 0.65 us
  matrix products: 13.5 us -> 0 us
  local copies, waits for them, and re-layouts: 10.5 us -> 5.33 us
    pallas_call x0 -> x1, Pallas kernels: none -> 153 us  [local(): pl.pallas_call(functools.partial(kernel, norm_scale), out_shape=(jax.Shap...]
    psum x1 -> x0, waiting for transfers between devices: 72.4 us -> none  [local(): weight_total, gain_total = lax.psum((weight_total, gain_total), 'rep')]
    all_gather x2 -> x0, waiting for transfers between devices: 71.4 us -> none  [local(): grads_all = lax.all_gather(grad_rows, 'fsdp', axis=0, tiled=True)]
    psum x2 -> x0, blocking collectives: 61.9 us -> none  [the longest x1 41.2 us: local(): lax.psum(jnp.sum(centered_gradient * centered_columns, axis=1), 'fsdp')]
    unnamed x1 -> x0, blocking collectives: 57.7 us -> none
    all_to_all x3 -> x0, waiting for transfers between devices: 36.1 us -> none  [the longest x2 27.3 us: local(): lax.all_to_all(layer_rows, 'fsdp', split_axis=1, concat_axis=0, tiled=True)]
    all_to_all x3 -> x0, starting transfers between devices: 26.6 us -> none  [the longest x2 18.3 us: local(): lax.all_to_all(layer_rows, 'fsdp', split_axis=1, concat_axis=0, tiled=True)]
    all_to_all x1 -> x0, blocking collectives: 21.5 us -> none  [local(): lax.all_to_all(local_cols, 'fsdp', split_axis=0, concat_axis=1, tiled=True)]
  transfers between devices with their start and end apart: 8 -> 0, of which waited for: 4 -> 0; matrix products, arithmetic and copies ran while one was open for 6% -> 0% of each run, Pallas kernels for 0% -> 0%
where the time goes in v1:
time: 160 us
  Pallas kernels  153 us (96%)
  local copies, waits for them, and re-layouts  5.33 us (3%)
    pallas_call x1, Pallas kernels, local(): pl.pallas_call(functools.partial(kernel, norm_scale), out_shape=(jax.Shap...  153 us
    unnamed x6, local copies, waits for them, and re-layouts  4.57 us

profile of v1, /device:TPU:4, one launch (start us, length us, event | category | flops | bytes accessed | tf_op | source)
XLA Modules:
  0.0 159.6 jit_solution(1089723959448247499)
XLA Ops:
  0.6 0.0 copy-start.1
  0.6 153.0 %relay.1 = (bf16[128,8192]{1,0:T(8,128)(2,1)}, f32[512,1024]{1,0:T(8,128)}, f32[8,128]{1,0:T(8,128)}) custom-call(bf16[128,8192]{1,0:T(8,128)(2,1)} %bitcast.7, bf16[128,1024]{1,0:T(8,128)(2,1)} %bitcast.12, bf16[512,1024]{1,0:T(8,128)(2,1)} %bitcast.11, bf16[1,512]{1,0:T(2,128)(2,1)} %gain_ref.1, bf16[128,8192]{1,0:T(8,128)(2,1)} %bitcast.8), custom_call_target="tpu_custom_call" | custom-call | tf_op jit(solution)/shard_map/relay/pallas_call | solution.py:391
  153.6 0.8 reshape.25
  154.4 0.0 copy-done.1
  154.4 0.6 convert_divide_fusion
  155.0 0.0 copy-start
  155.0 3.2 %copy.10 = bf16[1,2,64,8192]{3,2,1,0:T(8,128)(2,1)} copy(bf16[1,2,64,8192]{3,2,1,0:T(8,128)(2,1)} %bitcast.10) | data formatting | bytes 4194304
  158.2 0.0 copy-done
  158.2 1.3 copy.11
Async XLA Ops:
  0.6 153.8 %copy-start.1 = (bf16[1,512]{1,0:T(2,128)(2,1)S(1)}, bf16[1,512]{1,0:T(2,128)(2,1)}, u32[]{:S(2)}) copy-start(bf16[1,512]{1,0:T(2,128)(2,1)} %gain_ref.1) | copy-start | bytes 3076
  155.0 3.2 %copy-start = (f32[512,1024]{1,0:T(8,128)S(1)}, f32[512,1024]{1,0:T(8,128)}, u32[]{:S(2)}) copy-start(f32[512,1024]{1,0:T(8,128)} %get-tuple-element.7) | copy-start | bytes 6291460

commit v2 on v0

v2 whole, which is shorter than its diff:
```python
import functools

import jax
import jax.numpy as jnp
from jax import lax
from jax.experimental import pallas as pl
from jax.experimental.pallas import tpu as pltpu
from jax.sharding import PartitionSpec as P

NORM_EPS = 1e-05
MESH = pl.DeviceIdType.MESH
NZ = 8
NY = 4
F32 = jnp.float32
BF16 = jnp.bfloat16


def remote(src, dst, send_sem, recv_sem, device):
    return pltpu.make_async_remote_copy(
        src_ref=src, dst_ref=dst, send_sem=send_sem, recv_sem=recv_sem, device_id=device, device_id_type=MESH
    )


def kernel(
    norm_scale,
    x_hbm, g_hbm, w_hbm, gain_ref, top_hbm,
    ig_ref, wg_ref, gg_ref,
    xbuf, topbuf, wown, gain_src, gain_all, scale_buf, gx, acc_buf, nb, xr, gr, wr, pt, rt, po, pb, ra, sb, rb, db, dr, upper, ggbuf,
    local_sem, gain_ss, gain_rs, g_ss, g_rs, x_ss, x_rs, w_ss, w_rs, w2_ss, w2_rs, w3_ss, w3_rs,
    t_ss, t_rs,     a_ss, a_rs, b_ss, b_rs, c_ss, c_rs, q_ss, q_rs, d_ss, d_rs, u_ss, u_rs,
):
    tokens, width = xbuf.shape
    blocks, _, bw = gain_all.shape
    hw = bw // 2
    vw = gr.shape[1]
    rows = sb.shape[2]
    rep = lax.axis_index("rep")
    fs = lax.axis_index("fsdp")
    sec = lax.axis_index("section")
    xl, y, xh, z = rep % 2, rep // 2, fs // NZ, fs % NZ
    yp = (y + 1 + 2 * ((y + sec) % 2)) % NY
    zp = (z + 1 + (NZ - 2) * ((z + sec) % 2)) % NZ
    jy, jz = y % 2, z % 2
    xb = xh + sec * ((xl + xh) % 2 - xh)
    side = xl + sec * (xh - xl)
    twin = {"rep": y * 2 + 1 - xl, "fsdp": (xh + sec * (1 - 2 * xh)) * NZ + z}
    me = xb * 4 + jy * 2 + jz

    def half_of(label, i):
        return label[0] + sec * (i - label[0])

    def zprime(label, i):
        return label[2] + 2 * ((2 * label[1] + i + sec * ((label[0] + i) % 2 - i + 2)) % 4)

    def member(flip):
        fh, fy, fz = flip // 4, (flip // 2) % 2, flip % 2
        mxl = xl + fh * (1 - 2 * xl)
        mxh = xh + fh * (1 - sec) * (1 - 2 * xh)
        my = y + fy * (yp - y)
        mz = z + fz * (zp - z)
        label = (xb + fh * (1 - 2 * xb), my % 2, mz % 2)
        device = {"rep": my * 2 + mxl, "fsdp": mxh * NZ + mz}
        return device, label, label[0] * 4 + label[1] * 2 + label[2]

    def block(label, i):
        return half_of(label, i) * NZ + zprime(label, i)

    mine = (xb, jy, jz)

    def rows_of(m):
        return pl.ds(pl.multiple_of(m * tokens, tokens), tokens)

    my_rows = rows_of(me)
    other = (me + 4) % 8

    def columns(b):
        return pl.ds(pl.multiple_of(b * bw, bw), bw)

    xcopy = pltpu.make_async_copy(x_hbm, xbuf, local_sem.at[0])
    tcopy = pltpu.make_async_copy(top_hbm, topbuf, local_sem.at[1])
    wcopy = pltpu.make_async_copy(w_hbm, wown, local_sem.at[2])
    gcopy = pltpu.make_async_copy(g_hbm, gr.at[my_rows], local_sem.at[3])

    def local_start():
        for copy in (xcopy, gcopy, wcopy, tcopy):
            copy.start()
        gain_f = jnp.broadcast_to(gain_ref[...].astype(F32), gain_src.shape)
        gain_src[...] = gain_f
        gain_all[fs] = gain_f

    def meet():
        barrier = pltpu.get_barrier_semaphore()

        def hello(device):
            pl.semaphore_signal(barrier, inc=1, device_id=device, device_id_type=MESH)

        @pl.loop(1, 8)
        def _(f):
            hello(member(f)[0])
            hello({"rep": (rep + f) % 8})
            hello({"rep": (rep + f) % 8, "fsdp": (1 - xh) * NZ + z})

        @pl.loop(1, 16)
        def _(k):
            hello({"fsdp": (fs + k) % 16})

        hello({"section": 1 - sec})
        pl.semaphore_wait(barrier, 3 * 7 + 15 + 1)

    def gain_copy(k, owner):
        return remote(gain_src, gain_all.at[owner], gain_ss.at[k], gain_rs.at[owner], {"fsdp": (fs + k) % 16})

    def gains_start():
        @pl.loop(1, 16)
        def _(k):
            gain_copy(k, fs).start()

    def gains_wait():
        @pl.loop(1, 16)
        def _(k):
            gain_copy(k, (fs + k) % 16).wait_recv()

    def g_copy(n, f, owner, src):
        return remote(src, gr.at[rows_of(owner)], g_ss.at[n], g_rs.at[owner], member(f)[0])

    def grads_start():
        for n, f in enumerate((4, 1, 2, 3)):
            g_copy(n, f, me, g_hbm).start()

    def grads_pass():
        g_copy(0, 4, other, g_hbm).wait_recv()
        for n, f in enumerate((1, 2, 3)):
            g_copy(4 + n, f, other, gr.at[rows_of(other)]).start()

    def grads_wait():
        gcopy.wait()

        @pl.loop(1, 8)
        def _(f):
            @pl.when(f != 4)
            def _():
                g_copy(0, 4, member(f)[2], g_hbm).wait_recv()

    root = z == zprime(mine, side)
    wh = w_hbm.shape[0] // 2
    yh = y // 2

    def w_part(p):
        return pl.ds(pl.multiple_of(p * wh, wh), wh)

    def w_copy(n):
        return remote(
            w_hbm.at[w_part(yh)], wr.at[side, w_part(yh)], w_ss.at[n], w_rs.at[0],
            {"fsdp": xh * NZ + (z + (2, 6, 4)[n]) % NZ},
        )

    w_local = pltpu.make_async_copy(w_hbm.at[w_part(yh)], wr.at[side, w_part(yh)], local_sem.at[4])

    def w_across(p):
        return remote(
            wr.at[side, w_part(yh)], wr.at[side, w_part(p)], w2_ss.at[0], w2_rs.at[0], {"rep": ((y + 2) % NY) * 2 + xl}
        )

    def w_swap(n, p, owner):
        return remote(
            wr.at[side, w_part(p)], wr.at[owner, w_part(p)], w3_ss.at[n], w3_rs.at[p], twin
        )

    def weights_start():
        @pl.when(root)
        def _():
            w_local.start()
            for n in range(3):
                w_copy(n).start()

    def weights_across():
        @pl.when(root)
        def _():
            w_local.wait()

        @pl.when(jnp.logical_not(root))
        def _():
            w_copy(0).wait_recv()

        w_across(yh).start()
        w_swap(0, yh, side).start()

    def weights_pass():
        w_across(1 - yh).wait_recv()
        w_swap(1, 1 - yh, side).start()

    def swap_wait(p):
        w_swap(0, p, 1 - side).wait_recv()

    def scales():
        xcopy.wait()

        def squares(b, acc):
            v = xbuf[:, columns(b)].astype(F32)
            v = v * v
            for k in range(bw // 128):
                acc = acc + v[:, k * 128 : (k + 1) * 128]
            return acc

        acc = lax.fori_loop(0, blocks, squares, jnp.zeros((tokens, 128), F32))
        scale = lax.rsqrt(jnp.sum(acc, axis=1, keepdims=True) / width + NORM_EPS)
        scale_buf[...] = jnp.broadcast_to(scale, scale_buf.shape)

    def norm():
        @pl.loop(0, blocks)
        def _(b):
            v = xbuf[:, columns(b)].astype(F32) * scale_buf[:, 0:1]
            v = v * gain_all[b, 0:1, :]
            for h in range(2):
                gx[b, h] = v[:, h * hw : (h + 1) * hw]
                nb[b, h] = v[:, h * hw : (h + 1) * hw].astype(BF16)

    def x_copy(f, n, owner):
        device, label, _ = member(f)
        return remote(
            nb.at[block(label, n % 2), n // 2], xr.at[n, rows_of(owner)], x_ss.at[f, n], x_rs.at[owner, n], device
        )

    def normed_start(h):
        for i in range(2):
            n = 2 * h + i

            @pl.loop(1, 8)
            def _(f):
                x_copy(f, n, me).start()

            xr[n, my_rows] = nb[block(mine, i), h]

    def normed_wait(h):
        @pl.loop(1, 8)
        def _(f):
            for i in range(2):
                x_copy(f, 2 * h + i, member(f)[2]).wait_recv()

    def partial(n):
        return lax.dot_general(xr[n], gr[...], (((0,), (0,)), ((), ())), preferred_element_type=F32)

    def t_copy(h):
        return remote(pt.at[h], rt.at[h], t_ss.at[h], t_rs.at[h], twin)

    def wgrad_other(h):
        pt[h] = partial(2 * h + 1 - side).astype(BF16)
        t_copy(h).start()

    def wgrad_own(h):
        po[h] = partial(2 * h + side)

    def slice_of(c):
        return pl.ds(pl.multiple_of(c * rows, rows), rows)

    def a_copy(k, h, sender):
        c = (rep + k) % 8
        return remote(pb.at[h, slice_of(c)], ra.at[h, sender], a_ss.at[k, h], a_rs.at[sender, h], {"rep": c})

    def plane_start(h):
        t_copy(h).wait_recv()
        pb[h] = (po[h] + rt[h].astype(F32)).astype(BF16)

        @pl.loop(1, 8)
        def _(k):
            a_copy(k, h, rep).start()

        ra[h, rep] = pb[h, slice_of(rep)]

    def plane_wait(h):
        @pl.loop(1, 8)
        def _(k):
            a_copy(k, h, (rep + k) % 8).wait_recv()

    def plane_sum(h):
        for ky in range(2):
            for t in range(2):
                total = ra[h, 2 * ky + t].astype(F32) + ra[h, 2 * ky + 4 + t].astype(F32)
                sb[h, 2 * ky + t] = total.astype(BF16)

    def twin_sent():
        for h in range(2):
            t_copy(h).wait_send()

    zk = z // 2

    def b_copy(k, h, sender):
        slot = (zk + k) % 4
        return remote(
            sb.at[h, (slot + 2 * sec) % 4], rb.at[h, sender], b_ss.at[k, h], b_rs.at[sender, h],
            {"fsdp": xh * NZ + jz + 2 * slot},
        )

    def z_start(h):
        for k in range(1, 4):
            b_copy(k, h, zk).start()
        rb[h, zk] = sb[h, (zk + 2 * sec) % 4]

    def z_wait(h):
        for k in range(1, 4):
            b_copy(k, h, (zk + k) % 4).wait_recv()

    def out_rows(h, c):
        return pl.ds(pl.multiple_of(h * hw + c * rows, rows), rows)

    def z_sum(h):
        if h == 0:
            wcopy.wait()
        total = (rb[h, 0].astype(F32) + rb[h, 1].astype(F32)) + (rb[h, 2].astype(F32) + rb[h, 3].astype(F32))
        total = total * norm_scale
        wg_ref[out_rows(h, rep)] = total.astype(BF16)
        gg = jnp.sum(total * wown[out_rows(h, rep)].astype(F32), axis=1, keepdims=True)
        gg = jnp.broadcast_to(jnp.concatenate([gg] * (128 // rows), axis=0), (128, 128))
        ggbuf[h, rep] = gg.T[0:8]

    def c_copy(k, h, owner):
        part = wg_ref.at[out_rows(h, owner)]
        return remote(part, part, c_ss.at[k, h], c_rs.at[owner, h], {"rep": (rep + k) % 8})

    def q_copy(k, h, owner):
        part = ggbuf.at[h, owner]
        return remote(part, part, q_ss.at[k, h], q_rs.at[owner, h], {"rep": (rep + k) % 8})

    def gather_start(h):
        @pl.loop(1, 8)
        def _(k):
            c_copy(k, h, rep).start()
            q_copy(k, h, rep).start()

    def gather_wait(h):
        @pl.loop(1, 8)
        def _(k):
            c_copy(k, h, (rep + k) % 8).wait_recv()
            q_copy(k, h, (rep + k) % 8).wait_recv()

    def gradients_out():
        for h in range(2):
            for c in range(8):
                gg_ref[8 * h + c : 8 * h + c + 1] = ggbuf[h, c, 0:1]

    def d_copy(f, i, p, b):
        device, _, m = member(f)
        return remote(db.at[i, p, rows_of(m)], dr.at[b, p], d_ss.at[f, i, p], d_rs.at[b, p], device)

    def back_start(i, p):
        back = lax.dot_general(gr[...], wr[i, w_part(p)], (((1,), (1,)), ((), ())), preferred_element_type=F32)
        db[i, p] = back.astype(BF16)
        b = block(mine, i)

        @pl.loop(1, 8)
        def _(f):
            d_copy(f, i, p, b).start()

        dr[b, p] = db[i, p, my_rows]

    def first_half(f):
        return member(f)[0]["rep"] // 4

    def back_wait(n):
        @pl.loop(1, 8)
        def _(f):
            p = (first_half(f) + n) % 2
            for i in range(2):
                d_copy(f, i, p, block(member(f)[1], i)).wait_recv()

    def back_sent():
        @pl.loop(1, 8)
        def _(f):
            for i in range(2):
                for p in range(2):
                    d_copy(f, i, p, 0).wait_send()

    def dots(n):
        def add(f, acc):
            p = (first_half(f) + n) % 2
            for i in range(2):
                b = block(member(f)[1], i)
                v = dr[b, p].astype(F32) * gx[b, p]
                for k in range(hw // 128):
                    acc = acc + v[:, k * 128 : (k + 1) * 128]
            return acc

        start = jnp.zeros((tokens, 128), F32) if n == 0 else acc_buf[...]
        acc = lax.fori_loop(0, 8, add, start)
        if n == 0:
            acc_buf[...] = acc
        else:
            scale = scale_buf[:, 0:1]
            avg = jnp.sum(acc, axis=1, keepdims=True) / width
            acc_buf[...] = jnp.broadcast_to(scale * scale * avg, acc.shape)

    parts = u_ss.shape[0]
    part_rows = tokens // parts

    def part_of(n):
        return pl.ds(pl.multiple_of(n * part_rows, part_rows), part_rows)

    def u_copy(n):
        return remote(ig_ref.at[part_of(n)], upper.at[part_of(n)], u_ss.at[n], u_rs.at[n], {"section": 0})

    def owner():
        def finish(part, top):
            sc = scale_buf[part, :]
            c2 = acc_buf[part, :]

            @pl.loop(0, blocks)
            def _(b):
                for k in range(bw // 128):
                    lanes = slice(k * 128, (k + 1) * 128)
                    cols = pl.ds(pl.multiple_of(b * bw + k * 128, 128), 128)
                    half_lanes = slice(k * 128 % hw, k * 128 % hw + 128)
                    v = dr[b, k * 128 // hw, part, half_lanes].astype(F32) * gain_all[b, 0:1, lanes] * sc
                    v = (v - xbuf[part, cols].astype(F32) * c2).astype(BF16)
                    if top:
                        v = (topbuf[part, cols].astype(F32) + v.astype(F32)).astype(BF16)
                    ig_ref[part, cols] = v

        @pl.when(sec == 1)
        def _():
            @pl.loop(0, parts)
            def _(n):
                finish(part_of(n), True)
                u_copy(n).start()

        @pl.when(sec == 0)
        def _():
            @pl.loop(0, parts)
            def _(n):
                finish(part_of(n), False)

            @pl.loop(0, parts)
            def _(n):
                u_copy(n).wait_recv()
                part = part_of(n)
                for k in range(width // 1024):
                    cols = slice(k * 1024, (k + 1) * 1024)
                    v = upper[part, cols].astype(F32) + ig_ref[part, cols].astype(F32)
                    ig_ref[part, cols] = v.astype(BF16)

    def gains_sent():
        @pl.loop(1, 16)
        def _(k):
            gain_copy(k, fs).wait_send()

    def grads_sent():
        for n, f in enumerate((4, 1, 2, 3)):
            g_copy(n, f, me, g_hbm).wait_send()

    def passed_sent():
        for n, f in enumerate((1, 2, 3)):
            g_copy(4 + n, f, other, gr.at[rows_of(other)]).wait_send()

    def weights_sent():
        @pl.when(root)
        def _():
            for n in range(3):
                w_copy(n).wait_send()

    def across_sent():
        w_across(yh).wait_send()
        w_swap(0, yh, side).wait_send()

    def swap_sent():
        w_swap(1, 1 - yh, side).wait_send()

    def all_sent(copy, i, owner):
        @pl.loop(1, 8)
        def _(k):
            copy(k, i, owner).wait_send()

    def z_sent():
        for h in range(2):
            for k in range(1, 4):
                b_copy(k, h, zk).wait_send()

    def gather_sent():
        for h in range(2):
            all_sent(c_copy, h, rep)
            all_sent(q_copy, h, rep)

    def upper_sent():
        @pl.when(sec == 1)
        def _():
            @pl.loop(0, parts)
            def _(n):
                u_copy(n).wait_send()

    local_start()
    meet()
    gains_start()
    grads_start()
    scales()
    gains_wait()
    norm()
    grads_pass()
    normed_start(0)
    normed_start(1)
    grads_wait()
    normed_wait(0)
    wgrad_other(0)
    wgrad_own(0)
    normed_wait(1)
    weights_start()
    wgrad_other(1)
    plane_start(0)
    wgrad_own(1)
    plane_start(1)
    weights_across()
    back_start(side, yh)
    plane_wait(0)
    plane_sum(0)
    z_start(0)
    plane_wait(1)
    plane_sum(1)
    z_start(1)
    swap_wait(yh)
    back_start(1 - side, yh)
    weights_pass()
    back_start(side, 1 - yh)
    z_wait(0)
    z_sum(0)
    gather_start(0)
    z_wait(1)
    z_sum(1)
    gather_start(1)
    swap_wait(1 - yh)
    back_start(1 - side, 1 - yh)
    back_wait(0)
    dots(0)
    back_wait(1)
    dots(1)
    tcopy.wait()
    owner()
    gather_wait(0)
    gather_wait(1)
    gradients_out()
    gains_sent()
    grads_sent()
    passed_sent()
    weights_sent()
    across_sent()
    swap_sent()
    twin_sent()
    for i in range(2):
        all_sent(x_copy, i, me)
        all_sent(x_copy, 2 + i, me)
        all_sent(a_copy, i, rep)
    back_sent()
    z_sent()
    gather_sent()
    upper_sent()


def local(layer_input, value_grad, value_weight, norm_gain, top_grad):
    reps, groups = lax.axis_size("rep"), lax.axis_size("fsdp")
    _, micro, rows, width = layer_input.shape
    vw = value_grad.shape[3]
    tokens = micro * rows
    bw = value_weight.shape[1]
    blocks = width // bw
    slice_rows = bw // (2 * reps)
    norm_scale = float(tokens * reps * groups) ** (-0.5)
    hbm = pl.BlockSpec(memory_space=pltpu.HBM)
    vmem = pl.BlockSpec(memory_space=pltpu.VMEM)
    dma = pltpu.SemaphoreType.DMA
    grad, wgrad, ggrad = pl.pallas_call(
        functools.partial(kernel, norm_scale),
        out_shape=(
            pltpu.VMEM((tokens, width), BF16),
            pltpu.VMEM((bw, vw), BF16),
            pltpu.VMEM((16, 128), F32),
        ),
        in_specs=[hbm, hbm, hbm, vmem, hbm],
        out_specs=(vmem, vmem, vmem),
        scratch_shapes=[
            pltpu.VMEM((tokens, width), BF16),
            pltpu.VMEM((tokens, width), BF16),
            pltpu.VMEM((bw, vw), BF16),
            pltpu.VMEM((8, bw), F32),
            pltpu.VMEM((blocks, 8, bw), F32),
            pltpu.VMEM((tokens, 128), F32),
            pltpu.VMEM((blocks, 2, tokens, bw // 2), F32),
            pltpu.VMEM((tokens, 128), F32),
            pltpu.VMEM((blocks, 2, tokens, bw // 2), BF16),
            pltpu.VMEM((4, 8 * tokens, bw // 2), BF16),
            pltpu.VMEM((8 * tokens, vw), BF16),
            pltpu.VMEM((2, bw, vw), BF16),
            pltpu.VMEM((2, bw // 2, vw), BF16),
            pltpu.VMEM((2, bw // 2, vw), BF16),
            pltpu.VMEM((2, bw // 2, vw), F32),
            pltpu.VMEM((2, bw // 2, vw), BF16),
            pltpu.VMEM((2, 8, slice_rows, vw), BF16),
            pltpu.VMEM((2, 4, slice_rows, vw), BF16),
            pltpu.VMEM((2, 4, slice_rows, vw), BF16),
            pltpu.VMEM((2, 2, 8 * tokens, bw // 2), BF16),
            pltpu.VMEM((blocks, 2, tokens, bw // 2), BF16),
            pltpu.VMEM((tokens, width), BF16),
            pltpu.VMEM((2, 8, 8, 128), F32),
            dma((6,)),
            dma((16,)), dma((16,)),
            dma((7,)), dma((8,)),
            dma((8, 4)), dma((8, 4)),
            dma((3,)), dma((1,)), dma((1,)), dma((1,)), dma((2,)), dma((2,)),
            dma((2,)), dma((2,)),
            dma((8, 2)), dma((8, 2)),
            dma((4, 2)), dma((4, 2)),
            dma((8, 2)), dma((8, 2)), dma((8, 2)), dma((8, 2)),
            dma((8, 2, 2)), dma((16, 2)),
            dma((4,)), dma((4,)),
        ],
        compiler_params=pltpu.CompilerParams(
            collective_id=0, has_side_effects=True, vmem_limit_bytes=59 * 1024 * 1024
        ),
        name="relay",
    )(
        layer_input.reshape(tokens, width),
        value_grad.reshape(tokens, vw),
        value_weight[0],
        norm_gain,
        top_grad.reshape(tokens, width),
    )
    gain_grad = ggrad[:, :slice_rows].reshape(1, bw) / norm_gain.astype(F32)
    return grad.reshape(layer_input.shape), wgrad.astype(F32)[None], gain_grad


def solution(mesh):
    return jax.shard_map(
        local,
        mesh=mesh,
        in_specs=(
            P("section", None, ("rep", "fsdp"), None),
            P("section", None, ("rep", "fsdp"), None),
            P("section", "fsdp", None),
            P("section", "fsdp"),
            P(None, ("rep", "fsdp"), None),
        ),
        out_specs=(
            P("section", None, ("rep", "fsdp"), None),
            P("section", "fsdp", None),
            P("section", "fsdp"),
        ),
        check_vma=False,
    )
```

time: 408 us -> 120 us (0.29)
  the two profiles are of different devices: /device:TPU:4 before, /device:TPU:76 now
where the time goes in v2:
time: 120 us
  Pallas kernels  116 us (97%)
  other arithmetic  2.15 us (2%)
  local copies, waits for them, and re-layouts  1.41 us (1%)
    pallas_call x1, Pallas kernels, local(): pl.pallas_call(functools.partial(kernel, norm_scale), out_shape=(pltpu.VM...  116 us

profile of v2, /device:TPU:76, one launch (start us, length us, event | category | flops | bytes accessed | tf_op | source)
XLA Modules:
  0.0 120.3 jit_solution(17758917277990556934)
XLA Ops:
  0.6 116.0 %relay.1 = (bf16[128,8192]{1,0:T(8,128)(2,1)S(1)}, bf16[512,1024]{1,0:T(8,128)(2,1)S(1)}, f32[16,128]{1,0:T(8,128)S(1)}) custom-call(bf16[128,8192]{1,0:T(8,128)(2,1)} %bitcast.11, bf16[128,1024]{1,0:T(8,128)(2,1)} %bitcast.14, bf16[512,1024]{1,0:T(8,128)(2,1)} %bitcast.13, bf16[1,512]{1,0:T(2,128)(2,1)} %gain_ref.1, bf16[128,8192]{1,0:T(8,128)(2,1)} %bitcast.12), custom_call_target="tpu_custom_call" | custom-call | tf_op jit(solution)/shard_map/relay/pallas_call | solution.py:566
  116.7 0.0 copy-start
  116.7 1.3 %copy.9 = bf16[1,2,64,8192]{3,2,1,0:T(8,128)(2,1)} copy(bf16[1,2,64,8192]{3,2,1,0:T(8,128)(2,1)S(1)} %bitcast.9) | data formatting | bytes 4194304
  118.0 0.1 reshape.25
  118.1 0.0 copy-done
  118.1 0.6 convert_divide_fusion
  118.7 1.6 %bitcast_convert_fusion = f32[1,512,1024]{2,1,0:T(8,128)} fusion(bf16[512,1024]{1,0:T(8,128)(2,1)S(1)} %get-tuple-element.7), kind=kLoop, calls=%fused_computation | loop fusion | flops 524288 | bytes 3145728 | tf_op jit(solution)/shard_map/broadcast_in_dim | solution.py:623
Async XLA Ops:
  116.7 1.4 %copy-start = (bf16[1,512]{1,0:T(2,128)(2,1)S(1)}, bf16[1,512]{1,0:T(2,128)(2,1)}, u32[]{:S(2)}) copy-start(bf16[1,512]{1,0:T(2,128)(2,1)} %gain_ref.1) | copy-start | bytes 3076

commit v3 on v2

--- a/solution.py
+++ b/solution.py
@@ -9,6 +9,8 @@
 
 NORM_EPS = 1e-05
 MESH = pl.DeviceIdType.MESH
+CHUNKS = 4
+DEPTH = 1
 NZ = 8
 NY = 4
 F32 = jnp.float32
@@ -27,12 +29,12 @@
     ig_ref, wg_ref, gg_ref,
     xbuf, topbuf, wown, gain_src, gain_all, scale_buf, gx, acc_buf, nb, xr, gr, wr, pt, rt, po, pb, ra, sb, rb, db, dr, upper, ggbuf,
     local_sem, gain_ss, gain_rs, g_ss, g_rs, x_ss, x_rs, w_ss, w_rs, w2_ss, w2_rs, w3_ss, w3_rs,
-    t_ss, t_rs,     a_ss, a_rs, b_ss, b_rs, c_ss, c_rs, q_ss, q_rs, d_ss, d_rs, u_ss, u_rs,
+    t_ss, t_rs, a_ss, a_rs, b_ss, b_rs, c_ss, c_rs, q_ss, q_rs, d_ss, d_rs, u_ss, u_rs,
 ):
     tokens, width = xbuf.shape
-    blocks, _, bw = gain_all.shape
-    hw = bw // 2
-    vw = gr.shape[1]
+    bw, vw = w_hbm.shape
+    blocks, hw = width // bw, bw // 2
+    chunks, cw, _ = po.shape
     rows = sb.shape[2]
     rep = lax.axis_index("rep")
     fs = lax.axis_index("fsdp")
@@ -84,9 +86,11 @@
     def local_start():
         for copy in (xcopy, gcopy, wcopy, tcopy):
             copy.start()
-        gain_f = jnp.broadcast_to(gain_ref[...].astype(F32), gain_src.shape)
-        gain_src[...] = gain_f
-        gain_all[fs] = gain_f
+        gain_src[...] = jnp.zeros(gain_src.shape, F32)
+        ggbuf[rep] = jnp.zeros(ggbuf.shape[1:], F32)
+        for k in range(bw // 128):
+            gain_src[k : k + 1] = gain_ref[:, k * 128 : (k + 1) * 128].astype(F32)
+        gain_all[fs] = gain_src[...]
 
     def meet():
         barrier = pltpu.get_barrier_semaphore()
@@ -123,23 +127,30 @@
     def g_copy(n, f, owner, src):
         return remote(src, gr.at[rows_of(owner)], g_ss.at[n], g_rs.at[owner], member(f)[0])
 
+    def g_pass(n, f, flip):
+        owner = member(flip)[2]
+        return g_copy(n, f, owner, gr.at[rows_of(owner)])
+
     def grads_start():
-        for n, f in enumerate((4, 1, 2, 3)):
+        for n, f in enumerate((2, 1, 4)):
             g_copy(n, f, me, g_hbm).start()
 
-    def grads_pass():
-        g_copy(0, 4, other, g_hbm).wait_recv()
-        for n, f in enumerate((1, 2, 3)):
-            g_copy(4 + n, f, other, gr.at[rows_of(other)]).start()
+    def grads_over_z():
+        g_pass(3, 1, 2).wait_recv()
+        g_pass(3, 1, 2).start()
+        g_pass(4, 4, 2).start()
+
+    def grads_over_x():
+        for n, flip in ((5, 1), (6, 3)):
+            g_pass(n, 4, flip).wait_recv()
+            g_pass(n, 4, flip).start()
 
     def grads_wait():
         gcopy.wait()
 
-        @pl.loop(1, 8)
+        @pl.loop(4, 8)
         def _(f):
-            @pl.when(f != 4)
-            def _():
-                g_copy(0, 4, member(f)[2], g_hbm).wait_recv()
+            g_pass(0, 4, f).wait_recv()
 
     root = z == zprime(mine, side)
     wh = w_hbm.shape[0] // 2
@@ -209,11 +220,13 @@
     def norm():
         @pl.loop(0, blocks)
         def _(b):
-            v = xbuf[:, columns(b)].astype(F32) * scale_buf[:, 0:1]
-            v = v * gain_all[b, 0:1, :]
-            for h in range(2):
-                gx[b, h] = v[:, h * hw : (h + 1) * hw]
-                nb[b, h] = v[:, h * hw : (h + 1) * hw].astype(BF16)
+            for k in range(bw // 128):
+                lanes = slice(k * 128 % hw, k * 128 % hw + 128)
+                cols = pl.ds(pl.multiple_of(b * bw + k * 128, 128), 128)
+                v = xbuf[:, cols].astype(F32) * scale_buf[...]
+                v = v * gain_all[b, k : k + 1, :]
+                gx[b, k * 128 // hw, :, lanes] = v
+                nb[b, k * 128 // cw, :, k * 128 % cw : k * 128 % cw + 128] = v.astype(BF16)
 
     def x_copy(f, n, owner):
         device, label, _ = member(f)
@@ -227,6 +240,8 @@
 
             @pl.loop(1, 8)
             def _(f):
+                if h >= DEPTH:
+                    x_copy(f, n - 2 * DEPTH, me).wait_send()
                 x_copy(f, n, me).start()
 
             xr[n, my_rows] = nb[block(mine, i), h]
@@ -279,7 +294,7 @@
                 sb[h, 2 * ky + t] = total.astype(BF16)
 
     def twin_sent():
-        for h in range(2):
+        for h in range(chunks):
             t_copy(h).wait_send()
 
     zk = z // 2
@@ -301,7 +316,7 @@
             b_copy(k, h, (zk + k) % 4).wait_recv()
 
     def out_rows(h, c):
-        return pl.ds(pl.multiple_of(h * hw + c * rows, rows), rows)
+        return pl.ds(pl.multiple_of(h * cw + c * rows, rows), rows)
 
     def z_sum(h):
         if h == 0:
@@ -311,32 +326,29 @@
         wg_ref[out_rows(h, rep)] = total.astype(BF16)
         gg = jnp.sum(total * wown[out_rows(h, rep)].astype(F32), axis=1, keepdims=True)
         gg = jnp.broadcast_to(jnp.concatenate([gg] * (128 // rows), axis=0), (128, 128))
-        ggbuf[h, rep] = gg.T[0:8]
+        ggbuf[rep, h : h + 1] = gg.T[0:1]
 
     def c_copy(k, h, owner):
         part = wg_ref.at[out_rows(h, owner)]
         return remote(part, part, c_ss.at[k, h], c_rs.at[owner, h], {"rep": (rep + k) % 8})
 
-    def q_copy(k, h, owner):
-        part = ggbuf.at[h, owner]
-        return remote(part, part, q_ss.at[k, h], q_rs.at[owner, h], {"rep": (rep + k) % 8})
+    def q_copy(k, owner):
+        return remote(ggbuf.at[owner], ggbuf.at[owner], q_ss.at[k], q_rs.at[owner], {"rep": (rep + k) % 8})
 
     def gather_start(h):
         @pl.loop(1, 8)
         def _(k):
             c_copy(k, h, rep).start()
-            q_copy(k, h, rep).start()
-
-    def gather_wait(h):
-        @pl.loop(1, 8)
-        def _(k):
-            c_copy(k, h, (rep + k) % 8).wait_recv()
-            q_copy(k, h, (rep + k) % 8).wait_recv()
-
-    def gradients_out():
-        for h in range(2):
-            for c in range(8):
-                gg_ref[8 * h + c : 8 * h + c + 1] = ggbuf[h, c, 0:1]
+            if h == chunks - 1:
+                q_copy(k, rep).start()
+
+    def gather_wait():
+        @pl.loop(1, 8)
+        def _(k):
+            for h in range(chunks):
+                c_copy(k, h, (rep + k) % 8).wait_recv()
+            q_copy(k, (rep + k) % 8).wait_recv()
+        gg_ref[...] = ggbuf[...]
 
     def d_copy(f, i, p, b):
         device, _, m = member(f)
@@ -406,10 +418,9 @@
             @pl.loop(0, blocks)
             def _(b):
                 for k in range(bw // 128):
-                    lanes = slice(k * 128, (k + 1) * 128)
                     cols = pl.ds(pl.multiple_of(b * bw + k * 128, 128), 128)
                     half_lanes = slice(k * 128 % hw, k * 128 % hw + 128)
-                    v = dr[b, k * 128 // hw, part, half_lanes].astype(F32) * gain_all[b, 0:1, lanes] * sc
+                    v = dr[b, k * 128 // hw, part, half_lanes].astype(F32) * gain_all[b, k : k + 1, :] * sc
                     v = (v - xbuf[part, cols].astype(F32) * c2).astype(BF16)
                     if top:
                         v = (topbuf[part, cols].astype(F32) + v.astype(F32)).astype(BF16)
@@ -443,12 +454,8 @@
             gain_copy(k, fs).wait_send()
 
     def grads_sent():
-        for n, f in enumerate((4, 1, 2, 3)):
-            g_copy(n, f, me, g_hbm).wait_send()
-
-    def passed_sent():
-        for n, f in enumerate((1, 2, 3)):
-            g_copy(4 + n, f, other, gr.at[rows_of(other)]).wait_send()
+        for n in range(7):
+            g_copy(n, 4, me, g_hbm).wait_send()
 
     def weights_sent():
         @pl.when(root)
@@ -469,14 +476,17 @@
             copy(k, i, owner).wait_send()
 
     def z_sent():
-        for h in range(2):
+        for h in range(chunks):
             for k in range(1, 4):
                 b_copy(k, h, zk).wait_send()
 
     def gather_sent():
-        for h in range(2):
+        for h in range(chunks):
             all_sent(c_copy, h, rep)
-            all_sent(q_copy, h, rep)
+
+        @pl.loop(1, 8)
+        def _(k):
+            q_copy(k, rep).wait_send()
 
     def upper_sent():
         @pl.when(sec == 1)
@@ -490,39 +500,62 @@
     gains_start()
     grads_start()
     scales()
+    grads_over_z()
     gains_wait()
     norm()
-    grads_pass()
     normed_start(0)
     normed_start(1)
+    grads_over_x()
+    normed_start(2)
+    weights_start()
     grads_wait()
     normed_wait(0)
     wgrad_other(0)
+    normed_start(3)
     wgrad_own(0)
     normed_wait(1)
-    weights_start()
     wgrad_other(1)
     plane_start(0)
     wgrad_own(1)
+    normed_wait(2)
+    wgrad_other(2)
     plane_start(1)
     weights_across()
-    back_start(side, yh)
+    wgrad_own(2)
     plane_wait(0)
     plane_sum(0)
     z_start(0)
+    normed_wait(3)
+    wgrad_other(3)
+    plane_start(2)
+    wgrad_own(3)
     plane_wait(1)
     plane_sum(1)
     z_start(1)
-    swap_wait(yh)
-    back_start(1 - side, yh)
+    plane_start(3)
     weights_pass()
-    back_start(side, 1 - yh)
     z_wait(0)
     z_sum(0)
     gather_start(0)
+    back_start(side, yh)
+    plane_wait(2)
+    plane_sum(2)
+    z_start(2)
     z_wait(1)
     z_sum(1)
     gather_start(1)
+    plane_wait(3)
+    plane_sum(3)
+    z_start(3)
+    swap_wait(yh)
+    back_start(1 - side, yh)
+    z_wait(2)
+    z_sum(2)
+    gather_start(2)
+    back_start(side, 1 - yh)
+    z_wait(3)
+    z_sum(3)
+    gather_start(3)
     swap_wait(1 - yh)
     back_start(1 - side, 1 - yh)
     back_wait(0)
@@ -531,20 +564,18 @@
     dots(1)
     tcopy.wait()
     owner()
-    gather_wait(0)
-    gather_wait(1)
-    gradients_out()
+    gather_wait()
     gains_sent()
     grads_sent()
-    passed_sent()
     weights_sent()
     across_sent()
     swap_sent()
     twin_sent()
-    for i in range(2):
-        all_sent(x_copy, i, me)
-        all_sent(x_copy, 2 + i, me)
-        all_sent(a_copy, i, rep)
+    for h in range(chunks):
+        all_sent(a_copy, h, rep)
+        if h >= chunks - DEPTH:
+            all_sent(x_copy, 2 * h, me)
+            all_sent(x_copy, 2 * h + 1, me)
     back_sent()
     z_sent()
     gather_sent()
@@ -558,7 +589,8 @@
     tokens = micro * rows
     bw = value_weight.shape[1]
     blocks = width // bw
-    slice_rows = bw // (2 * reps)
+    cw = bw // CHUNKS
+    slice_rows = cw // reps
     norm_scale = float(tokens * reps * groups) ** (-0.5)
     hbm = pl.BlockSpec(memory_space=pltpu.HBM)
     vmem = pl.BlockSpec(memory_space=pltpu.VMEM)
@@ -568,7 +600,7 @@
         out_shape=(
             pltpu.VMEM((tokens, width), BF16),
             pltpu.VMEM((bw, vw), BF16),
-            pltpu.VMEM((16, 128), F32),
+            pltpu.VMEM((8, 8, 128), F32),
         ),
         in_specs=[hbm, hbm, hbm, vmem, hbm],
         out_specs=(vmem, vmem, vmem),
@@ -576,35 +608,35 @@
             pltpu.VMEM((tokens, width), BF16),
             pltpu.VMEM((tokens, width), BF16),
             pltpu.VMEM((bw, vw), BF16),
-            pltpu.VMEM((8, bw), F32),
-            pltpu.VMEM((blocks, 8, bw), F32),
+            pltpu.VMEM((8, 128), F32),
+            pltpu.VMEM((blocks, 8, 128), F32),
             pltpu.VMEM((tokens, 128), F32),
             pltpu.VMEM((blocks, 2, tokens, bw // 2), F32),
             pltpu.VMEM((tokens, 128), F32),
-            pltpu.VMEM((blocks, 2, tokens, bw // 2), BF16),
-            pltpu.VMEM((4, 8 * tokens, bw // 2), BF16),
+            pltpu.VMEM((blocks, CHUNKS, tokens, cw), BF16),
+            pltpu.VMEM((2 * CHUNKS, 8 * tokens, cw), BF16),
             pltpu.VMEM((8 * tokens, vw), BF16),
             pltpu.VMEM((2, bw, vw), BF16),
-            pltpu.VMEM((2, bw // 2, vw), BF16),
-            pltpu.VMEM((2, bw // 2, vw), BF16),
-            pltpu.VMEM((2, bw // 2, vw), F32),
-            pltpu.VMEM((2, bw // 2, vw), BF16),
-            pltpu.VMEM((2, 8, slice_rows, vw), BF16),
-            pltpu.VMEM((2, 4, slice_rows, vw), BF16),
-            pltpu.VMEM((2, 4, slice_rows, vw), BF16),
+            pltpu.VMEM((CHUNKS, cw, vw), BF16),
+            pltpu.VMEM((CHUNKS, cw, vw), BF16),
+            pltpu.VMEM((CHUNKS, cw, vw), F32),
+            pltpu.VMEM((CHUNKS, cw, vw), BF16),
+            pltpu.VMEM((CHUNKS, 8, slice_rows, vw), BF16),
+            pltpu.VMEM((CHUNKS, 4, slice_rows, vw), BF16),
+            pltpu.VMEM((CHUNKS, 4, slice_rows, vw), BF16),
             pltpu.VMEM((2, 2, 8 * tokens, bw // 2), BF16),
             pltpu.VMEM((blocks, 2, tokens, bw // 2), BF16),
             pltpu.VMEM((tokens, width), BF16),
-            pltpu.VMEM((2, 8, 8, 128), F32),
+            pltpu.VMEM((8, 8, 128), F32),
             dma((6,)),
             dma((16,)), dma((16,)),
             dma((7,)), dma((8,)),
-            dma((8, 4)), dma((8, 4)),
+            dma((8, 2 * CHUNKS)), dma((8, 2 * CHUNKS)),
             dma((3,)), dma((1,)), dma((1,)), dma((1,)), dma((2,)), dma((2,)),
-            dma((2,)), dma((2,)),
-            dma((8, 2)), dma((8, 2)),
-            dma((4, 2)), dma((4, 2)),
-            dma((8, 2)), dma((8, 2)), dma((8, 2)), dma((8, 2)),
+            dma((CHUNKS,)), dma((CHUNKS,)),
+            dma((8, CHUNKS)), dma((8, CHUNKS)),
+            dma((4, CHUNKS)), dma((4, CHUNKS)),
+            dma((8, CHUNKS)), dma((8, CHUNKS)), dma((8,)), dma((8,)),
             dma((8, 2, 2)), dma((16, 2)),
             dma((4,)), dma((4,)),
         ],
@@ -619,7 +651,7 @@
         norm_gain,
         top_grad.reshape(tokens, width),
     )
-    gain_grad = ggrad[:, :slice_rows].reshape(1, bw) / norm_gain.astype(F32)
+    gain_grad = ggrad[:, :CHUNKS, :slice_rows].swapaxes(0, 1).reshape(1, bw) / norm_gain.astype(F32)
     return grad.reshape(layer_input.shape), wgrad.astype(F32)[None], gain_grad
 
 

time: 120 us -> 109 us (0.908)
  the two profiles are of different devices: /device:TPU:76 before, /device:TPU:4 now
where the time goes in v3:
time: 109 us
  Pallas kernels  105 us (96%)
  other arithmetic  2.16 us (2%)
  local copies, waits for them, and re-layouts  1.42 us (1%)
    pallas_call x1, Pallas kernels, local(): pl.pallas_call(functools.partial(kernel, norm_scale), out_shape=(pltpu.VM...  105 us

profile of v3, /device:TPU:4, one launch (start us, length us, event | category | flops | bytes accessed | tf_op | source)
XLA Modules:
  0.0 109.1 jit_solution(1508426777005615603)
XLA Ops:
  0.6 104.9 %relay.1 = (bf16[128,8192]{1,0:T(8,128)(2,1)S(1)}, bf16[512,1024]{1,0:T(8,128)(2,1)S(1)}, f32[8,8,128]{2,1,0:T(8,128)S(1)}) custom-call(bf16[128,8192]{1,0:T(8,128)(2,1)} %bitcast.11, bf16[128,1024]{1,0:T(8,128)(2,1)} %bitcast.14, bf16[512,1024]{1,0:T(8,128)(2,1)} %bitcast.13, bf16[1,512]{1,0:T(2,128)(2,1)} %gain_ref.1, bf16[128,8192]{1,0:T(8,128)(2,1)} %bitcast.12), custom_call_target="tpu_custom_call" | custom-call | tf_op jit(solution)/shard_map/relay/pallas_call | solution.py:598
  105.5 0.0 copy-start
  105.5 1.3 %copy.10 = bf16[1,2,64,8192]{3,2,1,0:T(8,128)(2,1)} copy(bf16[1,2,64,8192]{3,2,1,0:T(8,128)(2,1)S(1)} %bitcast.10) | data formatting | bytes 4194304
  106.9 0.1 reshape.25
  106.9 0.0 copy-done
  106.9 0.6 convert_divide_fusion
  107.5 1.6 %bitcast_convert_fusion = f32[1,512,1024]{2,1,0:T(8,128)} fusion(bf16[512,1024]{1,0:T(8,128)(2,1)S(1)} %get-tuple-element.7), kind=kLoop, calls=%fused_computation | loop fusion | flops 524288 | bytes 3145728 | tf_op jit(solution)/shard_map/broadcast_in_dim | solution.py:655
  (2 shorter events, 0.0 us)
Async XLA Ops:
  105.5 1.4 %copy-start = (bf16[1,512]{1,0:T(2,128)(2,1)S(1)}, bf16[1,512]{1,0:T(2,128)(2,1)}, u32[]{:S(2)}) copy-start(bf16[1,512]{1,0:T(2,128)(2,1)} %gain_ref.1) | copy-start | bytes 3076

commit v4 on v3

--- a/solution.py
+++ b/solution.py
@@ -132,8 +132,9 @@
         return g_copy(n, f, owner, gr.at[rows_of(owner)])
 
     def grads_start():
+        gcopy.wait()
         for n, f in enumerate((2, 1, 4)):
-            g_copy(n, f, me, g_hbm).start()
+            g_copy(n, f, me, gr.at[my_rows]).start()
 
     def grads_over_z():
         g_pass(3, 1, 2).wait_recv()
@@ -146,8 +147,6 @@
             g_pass(n, 4, flip).start()
 
     def grads_wait():
-        gcopy.wait()
-
         @pl.loop(4, 8)
         def _(f):
             g_pass(0, 4, f).wait_recv()
@@ -161,7 +160,7 @@
 
     def w_copy(n):
         return remote(
-            w_hbm.at[w_part(yh)], wr.at[side, w_part(yh)], w_ss.at[n], w_rs.at[0],
+            wown.at[w_part(yh)], wr.at[side, w_part(yh)], w_ss.at[n], w_rs.at[0],
             {"fsdp": xh * NZ + (z + (2, 6, 4)[n]) % NZ},
         )
 
@@ -178,6 +177,8 @@
         )
 
     def weights_start():
+        wcopy.wait()
+
         @pl.when(root)
         def _():
             w_local.start()
@@ -241,8 +242,8 @@
             @pl.loop(1, 8)
             def _(f):
                 if h >= DEPTH:
-                    x_copy(f, n - 2 * DEPTH, me).wait_send()
-                x_copy(f, n, me).start()
+                    x_copy(8 - f, n - 2 * DEPTH, me).wait_send()
+                x_copy(8 - f, n, me).start()
 
             xr[n, my_rows] = nb[block(mine, i), h]
 
@@ -319,8 +320,6 @@
         return pl.ds(pl.multiple_of(h * cw + c * rows, rows), rows)
 
     def z_sum(h):
-        if h == 0:
-            wcopy.wait()
         total = (rb[h, 0].astype(F32) + rb[h, 1].astype(F32)) + (rb[h, 2].astype(F32) + rb[h, 3].astype(F32))
         total = total * norm_scale
         wg_ref[out_rows(h, rep)] = total.astype(BF16)
@@ -361,7 +360,7 @@
 
         @pl.loop(1, 8)
         def _(f):
-            d_copy(f, i, p, b).start()
+            d_copy(8 - f, i, p, b).start()
 
         dr[b, p] = db[i, p, my_rows]
 

time: 109 us -> 109 us (level)
  no operation moved by 1% of the time
where the time goes in v4:
time: 109 us
  Pallas kernels  104 us (95%)
  other arithmetic  2.16 us (2%)
  local copies, waits for them, and re-layouts  1.42 us (1%)
    pallas_call x1, Pallas kernels, local(): pl.pallas_call(functools.partial(kernel, norm_scale), out_shape=(pltpu.VM...  104 us

profile of v4, /device:TPU:4, one launch (start us, length us, event | category | flops | bytes accessed | tf_op | source)
XLA Modules:
  0.0 108.6 jit_solution(13749774200923578415)
XLA Ops:
  0.6 104.4 %relay.1 = (bf16[128,8192]{1,0:T(8,128)(2,1)S(1)}, bf16[512,1024]{1,0:T(8,128)(2,1)S(1)}, f32[8,8,128]{2,1,0:T(8,128)S(1)}) custom-call(bf16[128,8192]{1,0:T(8,128)(2,1)} %bitcast.11, bf16[128,1024]{1,0:T(8,128)(2,1)} %bitcast.14, bf16[512,1024]{1,0:T(8,128)(2,1)} %bitcast.13, bf16[1,512]{1,0:T(2,128)(2,1)} %gain_ref.1, bf16[128,8192]{1,0:T(8,128)(2,1)} %bitcast.12), custom_call_target="tpu_custom_call" | custom-call | tf_op jit(solution)/shard_map/relay/pallas_call | solution.py:597
  105.0 0.0 copy-start
  105.0 1.3 %copy.10 = bf16[1,2,64,8192]{3,2,1,0:T(8,128)(2,1)} copy(bf16[1,2,64,8192]{3,2,1,0:T(8,128)(2,1)S(1)} %bitcast.10) | data formatting | bytes 4194304
  106.4 0.1 reshape.25
  106.5 0.0 copy-done
  106.5 0.6 convert_divide_fusion
  107.1 1.6 %bitcast_convert_fusion = f32[1,512,1024]{2,1,0:T(8,128)} fusion(bf16[512,1024]{1,0:T(8,128)(2,1)S(1)} %get-tuple-element.7), kind=kLoop, calls=%fused_computation | loop fusion | flops 524288 | bytes 3145728 | tf_op jit(solution)/shard_map/broadcast_in_dim | solution.py:654
  (2 shorter events, 0.0 us)
Async XLA Ops:
  105.0 1.4 %copy-start = (bf16[1,512]{1,0:T(2,128)(2,1)S(1)}, bf16[1,512]{1,0:T(2,128)(2,1)}, u32[]{:S(2)}) copy-start(bf16[1,512]{1,0:T(2,128)(2,1)} %gain_ref.1) | copy-start | bytes 3076
